TPU v7x, 32 devices: a whole 2x2x4 slice. The times are simulated.
32 devices in a mesh: section: 2 (over core), dp: 8 (over z, y), mp: 2 (over x).
Axes of the slice: x: 2, y: 2, z: 4, core: 2. Of those that a mesh axis runs over, the one named last changes fastest.
Arguments:
- states: bfloat16 [2, 16, 128, 2816], P('section', 'dp'), may hold values from -8 to 8
- injection: bfloat16 [16, 128, 2816], P('dp', None, 'mp'), may hold values from -2.390625 to 2.390625
- cotangent: bfloat16 [16, 128, 2816], P('dp', None, 'mp'), may hold values from -6 to 6
- gain: float32 [2816], P('mp'), may hold values from 0.5 to 1.5
- weight: bfloat16 [2816, 2816], P(None, 'mp'), may hold values from -0.109375 to 0.109375
- exits: int32 [16], P('dp'), may hold values from 1 to 2, as said below
- order: int32 [8, 2], P('dp'), may hold values from 0 to 1, each once within a row
Outputs:
- d_injection: float32 [16, 128, 2816], P('dp', None, 'mp')
- d_weight: float32 [2816, 2816], P(('section', 'dp'), 'mp')
- d_gain: float32 [2816], P('mp')
Inputs may be any that keep to these rules, and one draw needn't show every extreme that they name: `exits`: some micro-batch runs all 2 iterations and some only one. `order`: each row is a permutation of 0 .. 1.
All inputs are finite; a program needn't handle non-finite values.
Results may differ from a plain program's by a relative error of at most 0.0033.
Values may be sent and summed in bfloat16 or wider, within the bound.
No kernel may reach another device: no remote copies, remote signals or barrier semaphores. Data moves between devices by JAX's collectives and lax.ppermute only.
A program may use at most 128 MiB of HBM per device.

v0:
```python
import jax
import jax.numpy as jnp
from jax import lax
from jax.experimental import pallas as pl
from jax.experimental.pallas import tpu as pltpu
from jax.sharding import PartitionSpec as P

epsilon = 1e-06
f32, bf16 = jnp.float32, jnp.bfloat16
VMEM = pl.BlockSpec(memory_space=pltpu.VMEM)
SMEM = pl.BlockSpec(memory_space=pltpu.SMEM)
HBM = pl.BlockSpec(memory_space=pltpu.HBM)


def call(kernel, outs, ins, scratch=(), limit=24):
    shapes = [jax.ShapeDtypeStruct(shape, kind) for shape, kind in outs]
    specs, values = zip(*ins)
    return pl.pallas_call(
        kernel,
        out_shape=shapes,
        in_specs=list(specs),
        out_specs=[VMEM] * len(shapes),
        scratch_shapes=list(scratch),
        compiler_params=pltpu.CompilerParams(vmem_limit_bytes=limit * 2**20),
        cost_estimate=pl.CostEstimate(flops=1000, bytes_accessed=1000, transcendentals=0),
    )(*values)


def swap(value, axis):
    return lax.ppermute(value, axis, [(0, 1), (1, 0)])


def opposite(value):
    return lax.ppermute(value, ("section", "mp"), [(i, 3 - i) for i in range(4)])


def own_slot():
    return lax.axis_index("section") ^ lax.axis_index("mp")


def chunks_of(total, size):
    return [(start, min(size, total - start)) for start in range(0, total, size)]


def to_rows(columns):
    rows = columns[0].shape[0]
    lane = lax.broadcasted_iota(jnp.int32, (rows, 128), 1)
    wide = jnp.zeros((rows, 128), f32)
    for index, column in enumerate(columns):
        wide = jnp.where(lane == index, column, wide)
    return wide.T[:8]


def to_columns(packed):
    return jnp.concatenate([packed] * 16, axis=0).T


def load(weight):
    parts = chunks_of(weight.shape[0], 512)

    def kernel(weight_hbm, w, sems):
        copies = []
        for index, (start, size) in enumerate(parts):
            part = pl.ds(start, size)
            copies.append(pltpu.make_async_copy(weight_hbm.at[part], w.at[part], sems.at[index]))
            copies[-1].start()
        for copy in copies:
            copy.wait()

    return call(
        kernel,
        [(weight.shape, bf16)],
        [(HBM, weight)],
        [pltpu.SemaphoreType.DMA((len(parts),))],
        limit=42,
    )[0]


def forward(stash, weight, injection, order, chips, group):
    slots, rows, features = stash.shape
    half = weight.shape[1]
    block = features // (2 * chips)
    groups = chips // group
    height = 2 * groups * block

    def kernel(order_ref, stash_ref, weight_ref, inj_ref, keep_ref, send_ref, *refs):
        *out_refs, turned, acc = refs
        slot = own_slot()
        left = stash_ref[...].reshape(slots * rows, features)
        for start, size in chunks_of(half, 256):
            part = slice(start, start + size)
            term = jnp.dot(left, weight_ref[:, part], preferred_element_type=f32)
            acc[:, :, part] = term.reshape(slots, rows, size)
        keep_ref[...] = acc[slot] + inj_ref[order_ref[0, slot]].astype(f32)
        send_ref[...] = acc[1 - slot] + inj_ref[order_ref[0, 1 - slot]].astype(f32)
        if out_refs:
            turned[...] = stash_ref[slot].T
        dp = lax.axis_index("dp")
        for distance, out_ref in enumerate(out_refs):
            for half_index in range(2):
                for other in range(groups):
                    chip = dp ^ (distance + group * other)
                    source = pl.multiple_of((half_index * chips + chip) * block, 16)
                    base = (half_index * groups + other) * block
                    out_ref[base : base + block] = turned[pl.ds(source, block)]

    pieces = group if block % 16 == 0 else 0
    keep, send, *columns = call(
        kernel,
        [((rows, half), f32)] * 2 + [((height, rows), bf16)] * pieces,
        [(SMEM, order), (VMEM, stash), (VMEM, weight), (VMEM, injection)],
        [pltpu.VMEM((features, rows), bf16), pltpu.VMEM((slots, rows, half), f32)],
    )
    if not columns:
        turned = lax.dynamic_index_in_dim(stash, own_slot(), 0, keepdims=False).T
        turned = turned.reshape(2, chips, block, rows)
        for distance in range(group):
            picked = [
                lax.dynamic_index_in_dim(
                    turned, lax.axis_index("dp") ^ (distance + group * other), 1, keepdims=False
                )
                for other in range(groups)
            ]
            columns.append(jnp.stack(picked, axis=1).reshape(height, rows))
    return keep, send, columns


def row_sums(order, cotangent, gain, keep, got):
    rows = keep.shape[0]

    def kernel(order_ref, cot_ref, gain_ref, keep_ref, got_ref, out_ref):
        sec = lax.axis_index("section")
        first = sec == 0
        keep, got = keep_ref[...], got_ref[...]
        pre1, pre0 = jnp.where(first, got, keep), jnp.where(first, keep, got)
        u = cot_ref[order_ref[0, own_slot()]].astype(f32) * gain_ref[...]
        sums = [pre1 * pre1, u * pre1, pre0 * pre0]
        out_ref[...] = to_rows([jnp.sum(each, axis=1, keepdims=True) for each in sums])

    ins = [(SMEM, order), (VMEM, cotangent), (VMEM, gain), (VMEM, keep), (VMEM, got)]
    return call(kernel, [((8, rows), f32)], ins)[0]


def delta_of(pre, u, squares, inner, features):
    radius = jnp.sqrt(squares / features + epsilon)
    inverse = 1.0 / radius
    normed = pre * inverse
    return normed, (u - normed * (inner * inverse / features)) * inverse


def lower_iteration1(order, exits, cotangent, gain, keep, got, sums, others, weight):
    rows, half = keep.shape
    features = weight.shape[0]

    def kernel(order_ref, exits_ref, cot_ref, gain_ref, keep_ref, got_ref, sums_ref, others_ref,
               weight_ref, db_ref, delta_ref, gain_out, away_ref):
        sec, mp = lax.axis_index("section"), lax.axis_index("mp")
        micro = order_ref[0, own_slot()]
        live = jnp.where(exits_ref[micro] > 1, 1.0, 0.0)
        stats = to_columns(sums_ref[...] + others_ref[...])
        pre = jnp.where(sec == 0, got_ref[...], keep_ref[...])
        cot = cot_ref[micro].astype(f32)
        normed, delta = delta_of(pre, cot * gain_ref[...], stats[:, 0:1], stats[:, 1:2], features)
        delta = delta * live
        delta_ref[...] = delta
        db = delta.astype(bf16)
        db_ref[...] = db
        gain_out[...] = jnp.sum(cot * normed, axis=0, keepdims=True) * live
        part = weight_ref[pl.ds(pl.multiple_of((1 - mp) * half, 128), half)]
        away_ref[...] = lax.dot_general(
            part, db, (((1,), (1,)), ((), ())), preferred_element_type=f32
        ).astype(bf16)

    return call(
        kernel,
        [((rows, half), bf16), ((rows, half), f32), ((1, half), f32), ((half, rows), bf16)],
        [(SMEM, order), (SMEM, exits), (VMEM, cotangent), (VMEM, gain), (VMEM, keep), (VMEM, got),
         (VMEM, sums), (VMEM, others), (VMEM, weight)],
    )


def kept_half(db, weight):
    rows, half = db.shape

    def kernel(db_ref, weight_ref, out_ref):
        part = weight_ref[pl.ds(pl.multiple_of(lax.axis_index("mp") * half, 128), half)]
        out_ref[...] = lax.dot_general(
            part, db_ref[...], (((1,), (1,)), ((), ())), preferred_element_type=f32
        )

    return call(kernel, [((half, rows), f32)], [(VMEM, db), (VMEM, weight)])[0]


def carry(order, exits, cotangent, gain, keep, got, sums, others, kept, sent, gain1, features):
    rows, half = keep.shape

    def kernel(order_ref, exits_ref, cot_ref, gain_ref, keep_ref, got_ref, sums_ref, others_ref,
               kept_ref, sent_ref, gain1_ref, carried_ref, inner_ref, gain_out):
        sec = lax.axis_index("section")
        micro = order_ref[0, own_slot()]
        passed = (kept_ref[...] + sent_ref[...].astype(f32)).astype(bf16).astype(f32).T
        cot = cot_ref[micro].astype(f32)
        carried = jnp.where(exits_ref[micro] > 1, passed, cot)
        carried_ref[...] = carried
        pre = jnp.where(sec == 0, keep_ref[...], got_ref[...])
        inner = jnp.sum(carried * gain_ref[...] * pre, axis=1, keepdims=True)
        inner_ref[...] = to_rows([inner])
        squares = to_columns(sums_ref[...] + others_ref[...])[:, 2:3]
        inverse = 1.0 / jnp.sqrt(squares / features + epsilon)
        gains = jnp.sum(carried * (pre * inverse), axis=0, keepdims=True) + gain1_ref[...]
        gain_out[...] = jnp.broadcast_to(gains, (8, half))

    return call(
        kernel,
        [((rows, half), f32), ((8, rows), f32), ((8, half), f32)],
        [(SMEM, order), (SMEM, exits)]
        + [
            (VMEM, value)
            for value in (cotangent, gain, keep, got, sums, others, kept, sent, gain1)
        ],
    )


def iteration0(gain, keep, got, sums, others, carried, inner, inner_other, delta1, features):
    rows, half = keep.shape

    def kernel(gain_ref, keep_ref, got_ref, sums_ref, others_ref, carried_ref, inner_ref, other_ref,
               delta1_ref, total_ref, db_ref):
        sec = lax.axis_index("section")
        squares = to_columns(sums_ref[...] + others_ref[...])[:, 2:3]
        inner = to_columns(inner_ref[...] + other_ref[...])[:, 0:1]
        pre = jnp.where(sec == 0, keep_ref[...], got_ref[...])
        _, delta = delta_of(pre, carried_ref[...] * gain_ref[...], squares, inner, features)
        total_ref[...] = delta + delta1_ref[...]
        db_ref[...] = delta.astype(bf16)

    values = [gain, keep, got, sums, others, carried, inner, inner_other, delta1]
    return call(
        kernel,
        [((rows, half), f32), ((rows, half), bf16)],
        [(VMEM, value) for value in values],
    )


def stacked(columns):
    def kernel(*refs):
        for chip, ref in enumerate(refs[:-1]):
            refs[-1][chip] = ref[...]

    outs = [((len(columns), *columns[0].shape), bf16)]
    return call(kernel, outs, [(VMEM, value) for value in columns])[0]


def left_side(columns, others):
    group, height, rows = columns.shape

    def kernel(own_ref, other_ref, out_ref):
        for index, pair in enumerate([(own_ref, other_ref), (other_ref, own_ref)]):

            @pl.when(lax.axis_index("section") == index)
            def _():
                for k, ref in enumerate(pair):
                    for chip in range(group):
                        base = (k * group + chip) * rows
                        out_ref[:, base : base + rows] = ref[chip]

    return call(
        kernel,
        [((height, 2 * group * rows), bf16)],
        [(VMEM, value) for value in (columns, others)],
    )[0]


def weight_terms(left, grads, k, lanes, base=()):
    rows = grads[0].shape[0]
    depth = len(grads) * rows
    height = left.shape[0]
    start, width = lanes

    def kernel(left_ref, *refs):
        grads_refs, base_refs = refs[: len(grads)], refs[len(grads) : -3]
        keep_ref, send_ref, right = refs[-3:]
        part = slice(start, start + width)
        for index, grads_ref in enumerate(grads_refs):
            right[index * rows : (index + 1) * rows] = grads_ref[:, part]
        for core, (first, second) in enumerate([(0, 1), (1, 0)]):

            @pl.when(lax.axis_index("section") == core)
            def _():
                terms = jnp.dot(
                    left_ref[:, k * depth : (k + 1) * depth],
                    right[...],
                    preferred_element_type=f32,
                )
                halves = [terms[: height // 2], terms[height // 2 :]]
                for out_ref, index in [(keep_ref, first), (send_ref, second)]:
                    total = halves[index]
                    if base_refs:
                        total = total + base_refs[0 if out_ref is keep_ref else 1][:, part]
                    out_ref[...] = total

    return call(
        kernel,
        [((height // 2, width), f32)] * 2,
        [(VMEM, value) for value in [left, *grads, *base]],
        [pltpu.VMEM((depth, width), bf16)],
    )


def chip_sum(keep, other, block):
    height, width = keep.shape

    def kernel(keep_ref, other_ref, own_ref, *away_refs):
        total = keep_ref[...] + other_ref[...]
        own_ref[...] = total[:block]
        for index, away_ref in enumerate(away_refs):
            away_ref[...] = total[(index + 1) * block : (index + 2) * block].astype(bf16)

    outs = [((block, width), f32)] + [((block, width), bf16)] * (height // block - 1)
    return call(kernel, outs, [(VMEM, keep), (VMEM, other)])


def final_sum(own, others, gains, half):
    block = own[0].shape[0]
    count = len(others[0])

    def kernel(*refs):
        gain_refs, refs = refs[: len(gains)], refs[len(gains) :]
        weight_out, gain_out = refs[-2:]
        start = 0
        for part in range(len(own)):
            own_ref, *other_refs = refs[part * (count + 1) : (part + 1) * (count + 1)]
            total = own_ref[...]
            for other_ref in other_refs:
                total = total + other_ref[...].astype(f32)
            width = own_ref.shape[1]
            weight_out[:, start : start + width] = total
            start += width
        sums = [ref[:1] for ref in gain_refs]
        while len(sums) > 1:
            sums = [a + b for a, b in zip(sums[::2], sums[1::2])]
        gain_out[...] = sums[0].reshape(half)

    values = [value for mine, theirs in zip(own, others) for value in (mine, *theirs)]
    ins = [(VMEM, value) for value in (*gains, *values)]
    return call(kernel, [((block, half), f32), ((half,), f32)], ins)


def place(order, total, other):
    rows, half = total.shape

    def kernel(order_ref, total_ref, other_ref, out_ref):
        micro = order_ref[0, own_slot()]
        out_ref[micro] = total_ref[...]
        out_ref[1 - micro] = other_ref[...]

    ins = [(SMEM, order), (VMEM, total), (VMEM, other)]
    return call(kernel, [((2, rows, half), f32)], ins)[0]


def shards(states, injection, cotangent, gain, weight, exits, order):
    stash = states[0]
    slots, rows, features = stash.shape
    half = weight.shape[1]
    dp = lax.axis_index("dp")
    chips = lax.axis_size("dp")
    group = 4
    groups = chips // group
    assert slots == 2 and lax.axis_size("section") == 2 and lax.axis_size("mp") == 2
    assert chips % group == 0 and groups & (groups - 1) == 0

    def across(value, distance):
        return lax.ppermute(value, "dp", [(i, i ^ distance) for i in range(chips)])

    def gathered(value):
        return [value] + [across(value, distance) for distance in range(1, group)]

    block = features // (2 * chips)
    gain = gain.reshape(1, half)
    weight = load(weight)
    keep, send, columns = forward(stash, weight, injection, order, chips, group)
    moved = [across(columns[distance], distance) for distance in range(group - 1, 0, -1)]
    columns = columns[:1] + moved[::-1]
    got = swap(send, "section")
    sums = row_sums(order, cotangent, gain, keep, got)
    others = opposite(sums)
    db1, delta1, gain1, away = lower_iteration1(
        order, exits, cotangent, gain, keep, got, sums, others, weight
    )
    blocks1, *moved = lax.optimization_barrier((db1, *columns[:0:-1]))
    columns = columns[:1] + moved[::-1]
    sent = opposite(away)
    grads1 = gathered(blocks1)
    kept = kept_half(db1, weight)
    kept, sent = lax.optimization_barrier((kept, sent))

    carried, inner, gains = carry(
        order, exits, cotangent, gain, keep, got, sums, others, kept, sent, gain1, features
    )
    inner_other, gains_other = opposite(inner), swap(gains, "section")
    columns = stacked(columns)
    gains = gains + gains_other
    total, db0 = iteration0(
        gain, keep, got, sums, others, carried, inner, inner_other, delta1, features
    )
    db0, gains, columns, *grads1[1:] = lax.optimization_barrier(
        (db0, gains, columns, *grads1[1:])
    )
    grads0 = gathered(db0)
    columns, total = lax.optimization_barrier((columns, total))
    left = left_side(columns, opposite(columns))

    far_gains = across(gains, 2)
    base = weight_terms(left, grads1, 1, (0, half))
    left, base, grads0, far_gains = lax.optimization_barrier((left, base, grads0, far_gains))
    gains = gains + far_gains

    cut = (half // 2 + 127) // 128 * 128
    terms = [
        weight_terms(left, grads0, 0, lanes, base) for lanes in [(0, cut), (cut, half - cut)]
    ]
    arrived = [swap(send, "section") for _, send in terms]
    own, others = [], []
    for part, (keep, _) in enumerate(terms):
        if part:
            keep, *_ = lax.optimization_barrier((keep, *aways))
            total, *_ = lax.optimization_barrier((total, *aways))
        mine, *aways = chip_sum(keep, arrived[part], block)
        own.append(mine)
        others.append([across(away, group * (i + 1)) for i, away in enumerate(aways)])
    gains, *_ = lax.optimization_barrier((gains, *aways))
    gains = gains + across(gains, 1)
    gains = [gains] + [across(gains, group * other) for other in range(1, groups)]
    d_injection = place(order, total, swap(total, "section"))
    others[1], d_injection = lax.optimization_barrier((others[1], d_injection))
    d_weight, d_gain = final_sum(own, others, gains, half)
    return (d_injection, d_weight, d_gain)


def solution(mesh):
    return jax.shard_map(
        shards,
        mesh=mesh,
        in_specs=(
            P("section", "dp", None, None),
            P("dp", None, "mp"),
            P("dp", None, "mp"),
            P("mp"),
            P(None, "mp"),
            P("dp"),
            P("dp", None),
        ),
        out_specs=(P("dp", None, "mp"), P(("section", "dp"), "mp"), P("mp")),
        check_vma=False,
    )
```

profile of v0, /device:TPU:0, one launch (start us, length us, event | category | flops | bytes accessed | tf_op | source)
XLA Modules:
  0.0 93.5 jit_solution(11348800230024648654)
XLA Ops:
  0.7 3.4 %shard_map.94.weight_ref = bf16[2816,1408]{1,0:T(8,128)(2,1)S(1)} custom-call(bf16[2816,1408]{1,0:T(8,128)(2,1)} %weight_hbm.1), custom_call_target="tpu_custom_call" | custom-call | flops 1000 | bytes 1000 | tf_op jit(solution)/shard_map/pallas_call | solution.py:18
  4.1 0.4 copy-done.1
  4.6 3.1 %shard_map.95 = (f32[128,1408]{1,0:T(8,128)S(1)}, f32[128,1408]{1,0:T(8,128)S(1)}, bf16[704,128]{1,0:T(8,128)(2,1)S(1)}, bf16[704,128]{1,0:T(8,128)(2,1)S(1)}, b...) custom-call(s32[1,2]{1,0:T(1,128)S(1)} %copy-done.3, bf16[2,128,2816]{2,1,0:T(8,128)(2,1)S(1)} %bitcast.1, ...), custom_call_target="tpu_custom_call" | custom-call | flops 1000 | bytes 1000 | tf_op jit(solution)/shard_map/pallas_call | solution.py:18
  7.7 0.0 copy-start.4
  7.7 0.5 collective-permute-start
  8.2 3.6 %collective-permute-start.5 = (bf16[704,128]{1,0:T(8,128)(2,1)S(1)}, bf16[704,128]{1,0:T(8,128)(2,1)S(1)}, u32[]{:S(2)}, u32[]{:S(2)}) collective-permute-start(bf16[704,128]{1,0:T(8,128)(2,1)S(1)} %get-tuple-element.70), channel_id=1, source_target_pairs={{0,6},{2,4},{4,2},{6,0},{8,14},{10,12},{12,10},{14,8},{1,7},{3,5},... | collective-permute-start | bytes 540680 | tf_op jit(solution)/shard_map/ppermute | solution.py:373
  11.8 0.5 collective-permute-start.6
  12.3 0.2 collective-permute-start.7
  12.5 0.0 copy-done.5
  12.5 0.0 collective-permute-done.got_ref
  12.5 0.9 shard_map.96.sums_ref
  13.4 1.0 %collective-permute-start.1 = (f32[8,128]{1,0:T(8,128)S(1)}, f32[8,128]{1,0:T(8,128)S(1)}, u32[]{:S(2)}, u32[]{:S(2)}) collective-permute-start(f32[8,128]{1,0:T(8,128)S(1)} %shard_map.96.sums_ref), channel_id=1, source_target_pairs={{0,17},{1,16},{16,1},{17,0},{2,19},{3,18},{18,3},{19,2},{4,21},{5,... | collective-permute-start | bytes 12296 | tf_op jit(solution)/shard_map/ppermute | solution.py:34
  14.4 2.0 %collective-permute-done.1.others_ref = f32[8,128]{1,0:T(8,128)S(1)} collective-permute-done((f32[8,128]{1,0:T(8,128)S(1)}, f32[8,128]{1,0:T(8,128)S(1)}, u32[]{:S(2)}, u32[]{:S(2)}) %collective-permute-start.1) | collective-permute-done | bytes 4128 | tf_op jit(solution)/shard_map/ppermute | solution.py:34
  16.5 2.1 %shard_map.97 = (bf16[128,1408]{1,0:T(8,128)(2,1)S(1)}, f32[128,1408]{1,0:T(8,128)S(1)}, f32[1,1408]{1,0:T(1,128)S(1)}, bf16[1408,128]{1,0:T(8,128)(2,1)S(1)}) custom-call(s32[1,2]{1,0:T(1,128)S(1)} %copy-done.3, s32[2]{0:T(128)S(1)} %copy-done.4, bf16[2,128,1408]{2,1,0:T(8,128)(2,1)S(1)} %copy-done, f32[1,1408]{1,0:T(1,128)S(1)} %reshape.9.gain_ref, ...), custom_call_target="tpu_custom_call" | custom-call | flops 1000 | bytes 1000 | tf_op jit(solution)/shard_map/pallas_call | solution.py:18
  18.5 1.4 %collective-permute-start.2 = (bf16[1408,128]{1,0:T(8,128)(2,1)S(1)}, bf16[1408,128]{1,0:T(8,128)(2,1)S(1)}, u32[]{:S(2)}, u32[]{:S(2)}) collective-permute-start(bf16[1408,128]{1,0:T(8,128)(2,1)S(1)} %get-tuple-element.60), channel_id=1, source_target_pairs={{0,17},{1,16},{16,1},{17,0},{2,19},{3,18},{18,3},{19,2},{4,21},{5,... | collective-permute-start | bytes 1081352 | tf_op jit(solution)/shard_map/ppermute | solution.py:34
  19.9 0.0 collective-permute-done.5.refs_3_
  19.9 1.1 %collective-permute-done.6.refs_2_ = bf16[704,128]{1,0:T(8,128)(2,1)S(1)} collective-permute-done((bf16[704,128]{1,0:T(8,128)(2,1)S(1)}, bf16[704,128]{1,0:T(8,128)(2,1)S(1)}, u32[]{:S(2)}, u32[]{:S(2)}) %collective-permute-start.6) | collective-permute-done | bytes 180256 | tf_op jit(solution)/shard_map/ppermute | solution.py:373
  21.0 0.0 collective-permute-done.7.refs_1_
  21.1 2.4 %collective-permute-start.10 = (bf16[128,1408]{1,0:T(8,128)(2,1)S(1)}, bf16[128,1408]{1,0:T(8,128)(2,1)S(1)}, u32[]{:S(2)}, u32[]{:S(2)}) collective-permute-start(bf16[128,1408]{1,0:T(8,128)(2,1)S(1)} %get-tuple-element.76.db_ref.refs_0_), channel_id=1, source_target_pairs={{0,6},{2,4},{4,2},{6,0},{8,14},{10,12},{12,10},{14,8},{1,7},{3,5},... | collective-permute-start | bytes 1081352 | tf_op jit(solution)/shard_map/ppermute | solution.py:373
  23.5 0.5 collective-permute-start.9
  23.9 0.6 collective-permute-start.8
  24.5 1.2 %shard_map.98.kept_ref = f32[1408,128]{1,0:T(8,128)S(1)} custom-call(bf16[128,1408]{1,0:T(8,128)(2,1)S(1)} %get-tuple-element.76.db_ref.refs_0_, bf16[2816,1408]{1,0:T(8,128)(2,1)S(1)} %shard_map.94.weight_ref), custom_call_target="tpu_custom_call" | custom-call | flops 1000 | bytes 1000 | tf_op jit(solution)/shard_map/pallas_call | solution.py:18
  25.7 3.0 %collective-permute-done.2.sent_ref = bf16[1408,128]{1,0:T(8,128)(2,1)S(1)} collective-permute-done((bf16[1408,128]{1,0:T(8,128)(2,1)S(1)}, bf16[1408,128]{1,0:T(8,128)(2,1)S(1)}, u32[]{:S(2)}, u32[]{:S(2)}) %collective-permute-start.2) | collective-permute-done | bytes 360480 | tf_op jit(solution)/shard_map/ppermute | solution.py:34
  28.7 1.0 %shard_map.99 = (f32[128,1408]{1,0:T(8,128)S(1)}, f32[8,128]{1,0:T(8,128)S(1)}, f32[8,1408]{1,0:T(8,128)S(1)}) custom-call(s32[1,2]{1,0:T(1,128)S(1)} %copy-done.3, s32[2]{0:T(128)S(1)} %copy-done.4, bf16[2,128,1408]{2,1,0:T(8,128)(2,1)S(1)} %copy-done, f32[1,1408]{1,0:T(1,128)S(1)} %reshape.9.gain_ref, f32[128,1408]{1,0:T(8,128)S(1)} %get-tuple-element.57.keep_ref, ...), custom_call_target="tpu_custom_call" | custom-call | flops 1000 | bytes 1000 | tf_op jit(solution)/shard_map/pallas_call | solution.py:18
  29.7 0.8 collective-permute-start.4
  30.5 1.7 %collective-permute-start.3 = (f32[8,128]{1,0:T(8,128)S(1)}, f32[8,128]{1,0:T(8,128)S(1)}, u32[]{:S(2)}, u32[]{:S(2)}) collective-permute-start(f32[8,128]{1,0:T(8,128)S(1)} %get-tuple-element.65.inner_ref), channel_id=1, source_target_pairs={{0,17},{1,16},{16,1},{17,0},{2,19},{3,18},{18,3},{19,2},{4,21},{5,... | collective-permute-start | bytes 12296 | tf_op jit(solution)/shard_map/ppermute | solution.py:34
  32.3 1.3 %collective-permute-done.3.other_ref = f32[8,128]{1,0:T(8,128)S(1)} collective-permute-done((f32[8,128]{1,0:T(8,128)S(1)}, f32[8,128]{1,0:T(8,128)S(1)}, u32[]{:S(2)}, u32[]{:S(2)}) %collective-permute-start.3) | collective-permute-done | bytes 4128 | tf_op jit(solution)/shard_map/ppermute | solution.py:34
  33.6 0.4 shard_map.100
  34.0 0.0 collective-permute-done.4
  34.0 0.0 collective-permute-done.10.refs_3_
  34.1 6.0 %collective-permute-done.9.refs_2_ = bf16[128,1408]{1,0:T(8,128)(2,1)S(1)} collective-permute-done((bf16[128,1408]{1,0:T(8,128)(2,1)S(1)}, bf16[128,1408]{1,0:T(8,128)(2,1)S(1)}, u32[]{:S(2)}, u32[]{:S(2)}) %collective-permute-start.9) | collective-permute-done | bytes 360480 | tf_op jit(solution)/shard_map/ppermute | solution.py:373
  40.0 0.0 collective-permute-done.8.refs_1_
  40.0 1.0 %collective-permute-start.11 = (bf16[4,704,128]{2,1,0:T(8,128)(2,1)S(1)}, bf16[4,704,128]{2,1,0:T(8,128)(2,1)S(1)}, u32[]{:S(2)}, u32[]{:S(2)}) collective-permute-start(bf16[4,704,128]{2,1,0:T(8,128)(2,1)S(1)} %shard_map.101.own_ref), channel_id=1, source_target_pairs={{0,17},{1,16},{16,1},{17,0},{2,19},{3,18},{18,3},{19,2},{4,21},{5,... | collective-permute-start | bytes 2162696 | tf_op jit(solution)/shard_map/ppermute | solution.py:34
  41.0 2.5 %collective-permute-start.14 = (bf16[128,1408]{1,0:T(8,128)(2,1)S(1)}, bf16[128,1408]{1,0:T(8,128)(2,1)S(1)}, u32[]{:S(2)}, u32[]{:S(2)}) collective-permute-start(bf16[128,1408]{1,0:T(8,128)(2,1)S(1)} %get-tuple-element.88.refs_0_), channel_id=1, source_target_pairs={{0,6},{2,4},{4,2},{6,0},{8,14},{10,12},{12,10},{14,8},{1,7},{3,5},... | collective-permute-start | bytes 1081352 | tf_op jit(solution)/shard_map/ppermute | solution.py:373
  43.5 0.5 collective-permute-start.13
  44.0 0.5 collective-permute-start.12
  44.5 1.6 %collective-permute-start.15 = (f32[8,1408]{1,0:T(8,128)S(1)}, f32[8,1408]{1,0:T(8,128)S(1)}, u32[]{:S(2)}, u32[]{:S(2)}) collective-permute-start(f32[8,1408]{1,0:T(8,128)S(1)} %add.9), channel_id=1, source_target_pairs={{0,4},{2,6},{4,0},{6,2},{8,12},{10,14},{12,8},{14,10},{1,5},{3,7},... | collective-permute-start | bytes 135176 | tf_op jit(solution)/shard_map/ppermute | solution.py:373
  46.1 12.3 %collective-permute-done.11.other_ref = bf16[4,704,128]{2,1,0:T(8,128)(2,1)S(1)} collective-permute-done((bf16[4,704,128]{2,1,0:T(8,128)(2,1)S(1)}, bf16[4,704,128]{2,1,0:T(8,128)(2,1)S(1)}, u32[]{:S(2)}, u32[]{:S(2)}) %collective-permute-start.11) | collective-permute-done | bytes 720928 | tf_op jit(solution)/shard_map/ppermute | solution.py:34
  58.4 0.4 shard_map.102.left_ref
  58.8 1.4 %shard_map.103 = (f32[352,1408]{1,0:T(8,128)S(1)}, f32[352,1408]{1,0:T(8,128)S(1)}) custom-call(bf16[704,1024]{1,0:T(8,128)(2,1)S(1)} %shard_map.102.left_ref, bf16[128,1408]{1,0:T(8,128)(2,1)S(1)} %get-tuple-element.76.db_ref.refs_0_, bf16[128,1408]{1,0:T(8,128)(2,1)S(1)} %collective-permute-done.8.refs_1_, ...), custom_call_target="tpu_custom_call" | custom-call | flops 1000 | bytes 1000 | tf_op jit(solution)/shard_map/pallas_call | solution.py:18
  60.2 1.3 %collective-permute-done.15 = f32[8,1408]{1,0:T(8,128)S(1)} collective-permute-done((f32[8,1408]{1,0:T(8,128)S(1)}, f32[8,1408]{1,0:T(8,128)S(1)}, u32[]{:S(2)}, u32[]{:S(2)}) %collective-permute-start.15) | collective-permute-done | bytes 45088 | tf_op jit(solution)/shard_map/ppermute | solution.py:373
  61.5 0.0 collective-permute-done.14.refs_3_
  61.5 0.0 collective-permute-done.13.refs_2_
  61.5 0.0 collective-permute-done.12.refs_1_
  61.5 0.8 shard_map.105
  62.3 0.1 collective-permute-start.16
  62.4 0.8 shard_map.104
  63.2 0.6 collective-permute-start.17
  63.7 1.4 %collective-permute-done.16.other_ref = f32[352,768]{1,0:T(8,128)S(1)} collective-permute-done((f32[352,768]{1,0:T(8,128)S(1)}, f32[352,768]{1,0:T(8,128)S(1)}, u32[]{:S(2)}, u32[]{:S(2)}) %collective-permute-start.16) | collective-permute-done | bytes 1081376 | tf_op jit(solution)/shard_map/ppermute | solution.py:30
  65.1 0.1 shard_map.106
  65.2 0.2 collective-permute-start.19
  65.4 2.6 %collective-permute-start.22 = (bf16[176,768]{1,0:T(8,128)(2,1)S(1)}, bf16[176,768]{1,0:T(8,128)(2,1)S(1)}, u32[]{:S(2)}, u32[]{:S(2)}) collective-permute-start(bf16[176,768]{1,0:T(8,128)(2,1)S(1)} %get-tuple-element.97), channel_id=1, source_target_pairs={{0,8},{2,10},{4,12},{6,14},{8,0},{10,2},{12,4},{14,6},{1,9},{3,11}... | collective-permute-start | bytes 811016 | tf_op jit(solution)/shard_map/ppermute | solution.py:373
  68.0 0.0 collective-permute-done.17.other_ref
  68.0 0.1 shard_map.107
  68.1 1.0 %collective-permute-start.18 = (bf16[176,640]{1,0:T(8,128)(2,1)S(1)}, bf16[176,640]{1,0:T(8,128)(2,1)S(1)}, u32[]{:S(2)}, u32[]{:S(2)}) collective-permute-start(bf16[176,640]{1,0:T(8,128)(2,1)S(1)} %get-tuple-element.100), channel_id=1, source_target_pairs={{0,8},{2,10},{4,12},{6,14},{8,0},{10,2},{12,4},{14,6},{1,9},{3,11}... | collective-permute-start | bytes 675848 | tf_op jit(solution)/shard_map/ppermute | solution.py:373
  69.2 0.6 collective-permute-start.20
  69.8 3.4 %collective-permute-done.20 = f32[8,1408]{1,0:T(8,128)S(1)} collective-permute-done((f32[8,1408]{1,0:T(8,128)S(1)}, f32[8,1408]{1,0:T(8,128)S(1)}, u32[]{:S(2)}, u32[]{:S(2)}) %collective-permute-start.20) | collective-permute-done | bytes 45088 | tf_op jit(solution)/shard_map/ppermute | solution.py:373
  73.2 2.0 %collective-permute-start.21 = (f32[8,1408]{1,0:T(8,128)S(1)}, f32[8,1408]{1,0:T(8,128)S(1)}, u32[]{:S(2)}, u32[]{:S(2)}) collective-permute-start(f32[8,1408]{1,0:T(8,128)S(1)} %add.11.refs_0_), channel_id=1, source_target_pairs={{0,8},{2,10},{4,12},{6,14},{8,0},{10,2},{12,4},{14,6},{1,9},{3,11}... | collective-permute-start | bytes 135176 | tf_op jit(solution)/shard_map/ppermute | solution.py:373
  75.3 0.0 collective-permute-done.19.other_ref
  75.3 1.7 %shard_map.108 = f32[2,128,1408]{2,1,0:T(8,128)} custom-call(s32[1,2]{1,0:T(1,128)S(1)} %copy-done.3, f32[128,1408]{1,0:T(8,128)S(1)} %get-tuple-element.102.total_ref, f32[128,1408]{1,0:T(8,128)S(1)} %collective-permute-done.19.other_ref), custom_call_target="tpu_custom_call" | custom-call | flops 1000 | bytes 1000 | tf_op jit(solution)/shard_map/pallas_call | solution.py:18
  77.0 14.9 %collective-permute-done.18.refs_5_ = bf16[176,640]{1,0:T(8,128)(2,1)S(1)} collective-permute-done((bf16[176,640]{1,0:T(8,128)(2,1)S(1)}, bf16[176,640]{1,0:T(8,128)(2,1)S(1)}, u32[]{:S(2)}, u32[]{:S(2)}) %collective-permute-start.18) | collective-permute-done | bytes 225312 | tf_op jit(solution)/shard_map/ppermute | solution.py:373
  92.0 0.5 collective-permute-done.21.refs_1_
  92.4 0.0 collective-permute-done.22.refs_3_
  92.4 1.0 %shard_map.109 = (f32[176,1408]{1,0:T(8,128)}, f32[1408]{0:T(1024)}) custom-call(f32[8,1408]{1,0:T(8,128)S(1)} %add.11.refs_0_, f32[8,1408]{1,0:T(8,128)S(1)} %collective-permute-done.21.refs_1_, f32[176,768]{1,0:T(8,128)S(1)} %get-tuple-element.106.refs_2_, bf16[176,768]{1,0:T(8,128)(2,1)S(1)} %collective-permute-done.22.refs_3_, ...), custom_call_target="tpu_custom_call" | custom-call | flops 1000 | bytes 1000 | tf_op jit(solution)/shard_map/pallas_call | solution.py:18
  (14 shorter events, 0.1 us)
Async XLA Ops:
  0.6 3.5 %copy-start.3 = (s32[1,2]{1,0:T(1,128)S(1)}, s32[1,2]{1,0:T(1,128)}, u32[]{:S(2)}) copy-start(s32[1,2]{1,0:T(1,128)} %order_ref.9) | copy-start | bytes 28
  0.6 3.5 %copy-start.2 = (bf16[2,128,1408]{2,1,0:T(8,128)(2,1)S(1)}, bf16[2,128,1408]{2,1,0:T(8,128)(2,1)}, u32[]{:S(2)}) copy-start(bf16[2,128,1408]{2,1,0:T(8,128)(2,1)} %inj_ref.1) | copy-start | bytes 2162692
  0.7 3.9 %copy-start.1 = (bf16[1,2,128,2816]{3,2,1,0:T(8,128)(2,1)S(1)}, bf16[1,2,128,2816]{3,2,1,0:T(8,128)(2,1)}, u32[]{:S(2)}) copy-start(bf16[1,2,128,2816]{3,2,1,0:T(8,128)(2,1)} %param.7) | copy-start | bytes 4325380
  4.6 7.9 %copy-start.5 = (f32[1408]{0:T(1024)S(1)}, f32[1408]{0:T(1024)}, u32[]{:S(2)}) copy-start(f32[1408]{0:T(1024)} %param.10) | copy-start | bytes 16900
  4.6 7.9 %copy-start = (bf16[2,128,1408]{2,1,0:T(8,128)(2,1)S(1)}, bf16[2,128,1408]{2,1,0:T(8,128)(2,1)}, u32[]{:S(2)}) copy-start(bf16[2,128,1408]{2,1,0:T(8,128)(2,1)} %cot_ref.5) | copy-start | bytes 2162692
  7.7 8.8 %copy-start.4 = (s32[2]{0:T(128)S(1)}, s32[2]{0:T(128)}, u32[]{:S(2)}) copy-start(s32[2]{0:T(128)} %exits_ref.3) | copy-start | bytes 28
  7.7 4.8 %collective-permute-start = (f32[128,1408]{1,0:T(8,128)S(1)}, f32[128,1408]{1,0:T(8,128)S(1)}, u32[]{:S(2)}, u32[]{:S(2)}) collective-permute-start(f32[128,1408]{1,0:T(8,128)S(1)} %get-tuple-element.58), channel_id=1, source_target_pairs={{0,16},{16,0},{1,17},{17,1},{2,18},{18,2},{3,19},{19,3},{4,20},{20... | collective-permute-start | bytes 2162696 | tf_op jit(solution)/shard_map/ppermute | solution.py:30
  8.2 11.7 %collective-permute-start.5 = (bf16[704,128]{1,0:T(8,128)(2,1)S(1)}, bf16[704,128]{1,0:T(8,128)(2,1)S(1)}, u32[]{:S(2)}, u32[]{:S(2)}) collective-permute-start(bf16[704,128]{1,0:T(8,128)(2,1)S(1)} %get-tuple-element.70), channel_id=1, source_target_pairs={{0,6},{2,4},{4,2},{6,0},{8,14},{10,12},{12,10},{14,8},{1,7},{3,5},... | collective-permute-start | bytes 540680 | tf_op jit(solution)/shard_map/ppermute | solution.py:373
  11.8 9.2 %collective-permute-start.6 = (bf16[704,128]{1,0:T(8,128)(2,1)S(1)}, bf16[704,128]{1,0:T(8,128)(2,1)S(1)}, u32[]{:S(2)}, u32[]{:S(2)}) collective-permute-start(bf16[704,128]{1,0:T(8,128)(2,1)S(1)} %get-tuple-element.71), channel_id=1, source_target_pairs={{0,4},{2,6},{4,0},{6,2},{8,12},{10,14},{12,8},{14,10},{1,5},{3,7},... | collective-permute-start | bytes 540680 | tf_op jit(solution)/shard_map/ppermute | solution.py:373
  12.3 8.8 %collective-permute-start.7 = (bf16[704,128]{1,0:T(8,128)(2,1)S(1)}, bf16[704,128]{1,0:T(8,128)(2,1)S(1)}, u32[]{:S(2)}, u32[]{:S(2)}) collective-permute-start(bf16[704,128]{1,0:T(8,128)(2,1)S(1)} %get-tuple-element.72), channel_id=1, source_target_pairs={{0,2},{2,0},{4,6},{6,4},{8,10},{10,8},{12,14},{14,12},{1,3},{3,1},... | collective-permute-start | bytes 540680 | tf_op jit(solution)/shard_map/ppermute | solution.py:373
  13.4 3.1 %collective-permute-start.1 = (f32[8,128]{1,0:T(8,128)S(1)}, f32[8,128]{1,0:T(8,128)S(1)}, u32[]{:S(2)}, u32[]{:S(2)}) collective-permute-start(f32[8,128]{1,0:T(8,128)S(1)} %shard_map.96.sums_ref), channel_id=1, source_target_pairs={{0,17},{1,16},{16,1},{17,0},{2,19},{3,18},{18,3},{19,2},{4,21},{5,... | collective-permute-start | bytes 12296 | tf_op jit(solution)/shard_map/ppermute | solution.py:34
  18.5 10.2 %collective-permute-start.2 = (bf16[1408,128]{1,0:T(8,128)(2,1)S(1)}, bf16[1408,128]{1,0:T(8,128)(2,1)S(1)}, u32[]{:S(2)}, u32[]{:S(2)}) collective-permute-start(bf16[1408,128]{1,0:T(8,128)(2,1)S(1)} %get-tuple-element.60), channel_id=1, source_target_pairs={{0,17},{1,16},{16,1},{17,0},{2,19},{3,18},{18,3},{19,2},{4,21},{5,... | collective-permute-start | bytes 1081352 | tf_op jit(solution)/shard_map/ppermute | solution.py:34
  21.1 13.0 %collective-permute-start.10 = (bf16[128,1408]{1,0:T(8,128)(2,1)S(1)}, bf16[128,1408]{1,0:T(8,128)(2,1)S(1)}, u32[]{:S(2)}, u32[]{:S(2)}) collective-permute-start(bf16[128,1408]{1,0:T(8,128)(2,1)S(1)} %get-tuple-element.76.db_ref.refs_0_), channel_id=1, source_target_pairs={{0,6},{2,4},{4,2},{6,0},{8,14},{10,12},{12,10},{14,8},{1,7},{3,5},... | collective-permute-start | bytes 1081352 | tf_op jit(solution)/shard_map/ppermute | solution.py:373
  23.5 16.5 %collective-permute-start.9 = (bf16[128,1408]{1,0:T(8,128)(2,1)S(1)}, bf16[128,1408]{1,0:T(8,128)(2,1)S(1)}, u32[]{:S(2)}, u32[]{:S(2)}) collective-permute-start(bf16[128,1408]{1,0:T(8,128)(2,1)S(1)} %get-tuple-element.76.db_ref.refs_0_), channel_id=1, source_target_pairs={{0,4},{2,6},{4,0},{6,2},{8,12},{10,14},{12,8},{14,10},{1,5},{3,7},... | collective-permute-start | bytes 1081352 | tf_op jit(solution)/shard_map/ppermute | solution.py:373
  23.9 16.1 %collective-permute-start.8 = (bf16[128,1408]{1,0:T(8,128)(2,1)S(1)}, bf16[128,1408]{1,0:T(8,128)(2,1)S(1)}, u32[]{:S(2)}, u32[]{:S(2)}) collective-permute-start(bf16[128,1408]{1,0:T(8,128)(2,1)S(1)} %get-tuple-element.76.db_ref.refs_0_), channel_id=1, source_target_pairs={{0,2},{2,0},{4,6},{6,4},{8,10},{10,8},{12,14},{14,12},{1,3},{3,1},... | collective-permute-start | bytes 1081352 | tf_op jit(solution)/shard_map/ppermute | solution.py:373
  29.7 4.3 %collective-permute-start.4 = (f32[8,1408]{1,0:T(8,128)S(1)}, f32[8,1408]{1,0:T(8,128)S(1)}, u32[]{:S(2)}, u32[]{:S(2)}) collective-permute-start(f32[8,1408]{1,0:T(8,128)S(1)} %get-tuple-element.68), channel_id=1, source_target_pairs={{0,16},{16,0},{1,17},{17,1},{2,18},{18,2},{3,19},{19,3},{4,20},{20... | collective-permute-start | bytes 135176 | tf_op jit(solution)/shard_map/ppermute | solution.py:30
  30.5 3.0 %collective-permute-start.3 = (f32[8,128]{1,0:T(8,128)S(1)}, f32[8,128]{1,0:T(8,128)S(1)}, u32[]{:S(2)}, u32[]{:S(2)}) collective-permute-start(f32[8,128]{1,0:T(8,128)S(1)} %get-tuple-element.65.inner_ref), channel_id=1, source_target_pairs={{0,17},{1,16},{16,1},{17,0},{2,19},{3,18},{18,3},{19,2},{4,21},{5,... | collective-permute-start | bytes 12296 | tf_op jit(solution)/shard_map/ppermute | solution.py:34
  40.0 18.4 %collective-permute-start.11 = (bf16[4,704,128]{2,1,0:T(8,128)(2,1)S(1)}, bf16[4,704,128]{2,1,0:T(8,128)(2,1)S(1)}, u32[]{:S(2)}, u32[]{:S(2)}) collective-permute-start(bf16[4,704,128]{2,1,0:T(8,128)(2,1)S(1)} %shard_map.101.own_ref), channel_id=1, source_target_pairs={{0,17},{1,16},{16,1},{17,0},{2,19},{3,18},{18,3},{19,2},{4,21},{5,... | collective-permute-start | bytes 2162696 | tf_op jit(solution)/shard_map/ppermute | solution.py:34
  41.0 20.5 %collective-permute-start.14 = (bf16[128,1408]{1,0:T(8,128)(2,1)S(1)}, bf16[128,1408]{1,0:T(8,128)(2,1)S(1)}, u32[]{:S(2)}, u32[]{:S(2)}) collective-permute-start(bf16[128,1408]{1,0:T(8,128)(2,1)S(1)} %get-tuple-element.88.refs_0_), channel_id=1, source_target_pairs={{0,6},{2,4},{4,2},{6,0},{8,14},{10,12},{12,10},{14,8},{1,7},{3,5},... | collective-permute-start | bytes 1081352 | tf_op jit(solution)/shard_map/ppermute | solution.py:373
  43.5 18.0 %collective-permute-start.13 = (bf16[128,1408]{1,0:T(8,128)(2,1)S(1)}, bf16[128,1408]{1,0:T(8,128)(2,1)S(1)}, u32[]{:S(2)}, u32[]{:S(2)}) collective-permute-start(bf16[128,1408]{1,0:T(8,128)(2,1)S(1)} %get-tuple-element.88.refs_0_), channel_id=1, source_target_pairs={{0,4},{2,6},{4,0},{6,2},{8,12},{10,14},{12,8},{14,10},{1,5},{3,7},... | collective-permute-start | bytes 1081352 | tf_op jit(solution)/shard_map/ppermute | solution.py:373
  44.0 17.5 %collective-permute-start.12 = (bf16[128,1408]{1,0:T(8,128)(2,1)S(1)}, bf16[128,1408]{1,0:T(8,128)(2,1)S(1)}, u32[]{:S(2)}, u32[]{:S(2)}) collective-permute-start(bf16[128,1408]{1,0:T(8,128)(2,1)S(1)} %get-tuple-element.88.refs_0_), channel_id=1, source_target_pairs={{0,2},{2,0},{4,6},{6,4},{8,10},{10,8},{12,14},{14,12},{1,3},{3,1},... | collective-permute-start | bytes 1081352 | tf_op jit(solution)/shard_map/ppermute | solution.py:373
  44.5 17.0 %collective-permute-start.15 = (f32[8,1408]{1,0:T(8,128)S(1)}, f32[8,1408]{1,0:T(8,128)S(1)}, u32[]{:S(2)}, u32[]{:S(2)}) collective-permute-start(f32[8,1408]{1,0:T(8,128)S(1)} %add.9), channel_id=1, source_target_pairs={{0,4},{2,6},{4,0},{6,2},{8,12},{10,14},{12,8},{14,10},{1,5},{3,7},... | collective-permute-start | bytes 135176 | tf_op jit(solution)/shard_map/ppermute | solution.py:373
  62.3 2.8 %collective-permute-start.16 = (f32[352,768]{1,0:T(8,128)S(1)}, f32[352,768]{1,0:T(8,128)S(1)}, u32[]{:S(2)}, u32[]{:S(2)}) collective-permute-start(f32[352,768]{1,0:T(8,128)S(1)} %get-tuple-element.96), channel_id=1, source_target_pairs={{0,16},{16,0},{1,17},{17,1},{2,18},{18,2},{3,19},{19,3},{4,20},{20... | collective-permute-start | bytes 3244040 | tf_op jit(solution)/shard_map/ppermute | solution.py:30
  63.2 4.8 %collective-permute-start.17 = (f32[352,640]{1,0:T(8,128)S(1)}, f32[352,640]{1,0:T(8,128)S(1)}, u32[]{:S(2)}, u32[]{:S(2)}) collective-permute-start(f32[352,640]{1,0:T(8,128)S(1)} %get-tuple-element.99), channel_id=1, source_target_pairs={{0,16},{16,0},{1,17},{17,1},{2,18},{18,2},{3,19},{19,3},{4,20},{20... | collective-permute-start | bytes 2703368 | tf_op jit(solution)/shard_map/ppermute | solution.py:30
  65.2 10.1 %collective-permute-start.19 = (f32[128,1408]{1,0:T(8,128)S(1)}, f32[128,1408]{1,0:T(8,128)S(1)}, u32[]{:S(2)}, u32[]{:S(2)}) collective-permute-start(f32[128,1408]{1,0:T(8,128)S(1)} %get-tuple-element.102.total_ref), channel_id=1, source_target_pairs={{0,16},{16,0},{1,17},{17,1},{2,18},{18,2},{3,19},{19,3},{4,20},{20... | collective-permute-start | bytes 2162696 | tf_op jit(solution)/shard_map/ppermute | solution.py:30
  65.4 27.0 %collective-permute-start.22 = (bf16[176,768]{1,0:T(8,128)(2,1)S(1)}, bf16[176,768]{1,0:T(8,128)(2,1)S(1)}, u32[]{:S(2)}, u32[]{:S(2)}) collective-permute-start(bf16[176,768]{1,0:T(8,128)(2,1)S(1)} %get-tuple-element.97), channel_id=1, source_target_pairs={{0,8},{2,10},{4,12},{6,14},{8,0},{10,2},{12,4},{14,6},{1,9},{3,11}... | collective-permute-start | bytes 811016 | tf_op jit(solution)/shard_map/ppermute | solution.py:373
  68.1 23.8 %collective-permute-start.18 = (bf16[176,640]{1,0:T(8,128)(2,1)S(1)}, bf16[176,640]{1,0:T(8,128)(2,1)S(1)}, u32[]{:S(2)}, u32[]{:S(2)}) collective-permute-start(bf16[176,640]{1,0:T(8,128)(2,1)S(1)} %get-tuple-element.100), channel_id=1, source_target_pairs={{0,8},{2,10},{4,12},{6,14},{8,0},{10,2},{12,4},{14,6},{1,9},{3,11}... | collective-permute-start | bytes 675848 | tf_op jit(solution)/shard_map/ppermute | solution.py:373
  69.2 4.0 %collective-permute-start.20 = (f32[8,1408]{1,0:T(8,128)S(1)}, f32[8,1408]{1,0:T(8,128)S(1)}, u32[]{:S(2)}, u32[]{:S(2)}) collective-permute-start(f32[8,1408]{1,0:T(8,128)S(1)} %add.10), channel_id=1, source_target_pairs={{0,2},{2,0},{4,6},{6,4},{8,10},{10,8},{12,14},{14,12},{1,3},{3,1},... | collective-permute-start | bytes 135176 | tf_op jit(solution)/shard_map/ppermute | solution.py:373
  73.2 19.2 %collective-permute-start.21 = (f32[8,1408]{1,0:T(8,128)S(1)}, f32[8,1408]{1,0:T(8,128)S(1)}, u32[]{:S(2)}, u32[]{:S(2)}) collective-permute-start(f32[8,1408]{1,0:T(8,128)S(1)} %add.11.refs_0_), channel_id=1, source_target_pairs={{0,8},{2,10},{4,12},{6,14},{8,0},{10,2},{12,4},{14,6},{1,9},{3,11}... | collective-permute-start | bytes 135176 | tf_op jit(solution)/shard_map/ppermute | solution.py:373
where the time goes:
time: 93.7 us; the launch traced here: 93.5 us
  waiting for transfers between devices  47.2 us (50%)
  starting transfers between devices  26.3 us (28%)
  Pallas kernels  18.6 us (20%)
    ppermute x14, waiting for transfers between devices, across(): return lax.ppermute(value, 'dp', [(i, i ^ distance) for i in range(chips)])  27.3 us
    ppermute x14, starting transfers between devices, across(): return lax.ppermute(value, 'dp', [(i, i ^ distance) for i in range(chips)])  19.1 us
    pallas_call x16, Pallas kernels, call(): pl.pallas_call(kernel, out_shape=shapes, in_specs=list(specs), out_specs=...  18.6 us
    ppermute x4, waiting for transfers between devices, opposite(): lax.ppermute(value, ('section', 'mp'), [(i, 3 - i) for i in range(4)])  18.6 us
    ppermute x4, starting transfers between devices, opposite(): lax.ppermute(value, ('section', 'mp'), [(i, 3 - i) for i in range(4)])  5.13 us
    ppermute x5, starting transfers between devices, swap(): return lax.ppermute(value, axis, [(0, 1), (1, 0)])  2.13 us
  transfers between devices with their start and end apart: 23, of which 11 were waited for; matrix products, arithmetic and copies ran while one was open for 0% of the time, Pallas kernels for 11%

commit v1 on v0

--- a/solution.py
+++ b/solution.py
@@ -56,7 +56,7 @@
 
 
 def load(weight):
-    parts = chunks_of(weight.shape[0], 512)
+    parts = chunks_of(weight.shape[0], 176)
 
     def kernel(weight_hbm, w, sems):
         copies = []
@@ -84,15 +84,16 @@
     height = 2 * groups * block
 
     def kernel(order_ref, stash_ref, weight_ref, inj_ref, keep_ref, send_ref, *refs):
-        *out_refs, turned, acc = refs
+        *out_refs, turned = refs
         slot = own_slot()
         left = stash_ref[...].reshape(slots * rows, features)
         for start, size in chunks_of(half, 256):
             part = slice(start, start + size)
             term = jnp.dot(left, weight_ref[:, part], preferred_element_type=f32)
-            acc[:, :, part] = term.reshape(slots, rows, size)
-        keep_ref[...] = acc[slot] + inj_ref[order_ref[0, slot]].astype(f32)
-        send_ref[...] = acc[1 - slot] + inj_ref[order_ref[0, 1 - slot]].astype(f32)
+            first, second = term[:rows], term[rows:]
+            keep, send = jnp.where(slot == 0, first, second), jnp.where(slot == 0, second, first)
+            keep_ref[:, part] = keep + inj_ref[order_ref[0, slot], :, part].astype(f32)
+            send_ref[:, part] = send + inj_ref[order_ref[0, 1 - slot], :, part].astype(f32)
         if out_refs:
             turned[...] = stash_ref[slot].T
         dp = lax.axis_index("dp")
@@ -109,7 +110,7 @@
         kernel,
         [((rows, half), f32)] * 2 + [((height, rows), bf16)] * pieces,
         [(SMEM, order), (VMEM, stash), (VMEM, weight), (VMEM, injection)],
-        [pltpu.VMEM((features, rows), bf16), pltpu.VMEM((slots, rows, half), f32)],
+        [pltpu.VMEM((features, rows), bf16)],
     )
     if not columns:
         turned = lax.dynamic_index_in_dim(stash, own_slot(), 0, keepdims=False).T

time: 93.7 us -> 93.6 us (level)
  no operation moved by 1% of the time
where the time goes in v1:
time: 93.6 us; the launch traced here: 93.4 us
  waiting for transfers between devices  47.2 us (50%)
  starting transfers between devices  26.3 us (28%)
  Pallas kernels  18.6 us (20%)
    ppermute x14, waiting for transfers between devices, across(): return lax.ppermute(value, 'dp', [(i, i ^ distance) for i in range(chips)])  27.3 us
    ppermute x14, starting transfers between devices, across(): return lax.ppermute(value, 'dp', [(i, i ^ distance) for i in range(chips)])  19.1 us
    pallas_call x16, Pallas kernels, call(): pl.pallas_call(kernel, out_shape=shapes, in_specs=list(specs), out_specs=...  18.6 us
    ppermute x4, waiting for transfers between devices, opposite(): lax.ppermute(value, ('section', 'mp'), [(i, 3 - i) for i in range(4)])  18.6 us
    ppermute x4, starting transfers between devices, opposite(): lax.ppermute(value, ('section', 'mp'), [(i, 3 - i) for i in range(4)])  5.14 us
    ppermute x5, starting transfers between devices, swap(): return lax.ppermute(value, axis, [(0, 1), (1, 0)])  2.14 us
  transfers between devices with their start and end apart: 23, of which 11 were waited for; matrix products, arithmetic and copies ran while one was open for 0% of the time, Pallas kernels for 11%

profile of v1, /device:TPU:0, one launch (start us, length us, event | category | flops | bytes accessed | tf_op | source)
XLA Modules:
  0.0 93.4 jit_solution(4847619603188000900)
XLA Ops:
  0.6 0.0 copy-start.3
  0.7 3.5 %shard_map.94.weight_ref = bf16[2816,1408]{1,0:T(8,128)(2,1)S(1)} custom-call(bf16[2816,1408]{1,0:T(8,128)(2,1)} %weight_hbm.1), custom_call_target="tpu_custom_call" | custom-call | flops 1000 | bytes 1000 | tf_op jit(solution)/shard_map/pallas_call | solution.py:18
  4.2 0.4 copy-done.1
  4.6 3.0 %shard_map.95 = (f32[128,1408]{1,0:T(8,128)S(1)}, f32[128,1408]{1,0:T(8,128)S(1)}, bf16[704,128]{1,0:T(8,128)(2,1)S(1)}, bf16[704,128]{1,0:T(8,128)(2,1)S(1)}, b...) custom-call(s32[1,2]{1,0:T(1,128)S(1)} %copy-done.3, bf16[2,128,2816]{2,1,0:T(8,128)(2,1)S(1)} %bitcast.1, ...), custom_call_target="tpu_custom_call" | custom-call | flops 1000 | bytes 1000 | tf_op jit(solution)/shard_map/pallas_call | solution.py:18
  7.6 0.0 copy-start.4
  7.6 0.5 collective-permute-start
  8.1 3.6 %collective-permute-start.5 = (bf16[704,128]{1,0:T(8,128)(2,1)S(1)}, bf16[704,128]{1,0:T(8,128)(2,1)S(1)}, u32[]{:S(2)}, u32[]{:S(2)}) collective-permute-start(bf16[704,128]{1,0:T(8,128)(2,1)S(1)} %get-tuple-element.70), channel_id=1, source_target_pairs={{0,6},{2,4},{4,2},{6,0},{8,14},{10,12},{12,10},{14,8},{1,7},{3,5},... | collective-permute-start | bytes 540680 | tf_op jit(solution)/shard_map/ppermute | solution.py:374
  11.7 0.4 collective-permute-start.6
  12.2 0.2 collective-permute-start.7
  12.4 0.0 collective-permute-done.got_ref
  12.4 0.9 shard_map.96.sums_ref
  13.3 1.0 %collective-permute-start.1 = (f32[8,128]{1,0:T(8,128)S(1)}, f32[8,128]{1,0:T(8,128)S(1)}, u32[]{:S(2)}, u32[]{:S(2)}) collective-permute-start(f32[8,128]{1,0:T(8,128)S(1)} %shard_map.96.sums_ref), channel_id=1, source_target_pairs={{0,17},{1,16},{16,1},{17,0},{2,19},{3,18},{18,3},{19,2},{4,21},{5,... | collective-permute-start | bytes 12296 | tf_op jit(solution)/shard_map/ppermute | solution.py:34
  14.4 2.0 %collective-permute-done.1.others_ref = f32[8,128]{1,0:T(8,128)S(1)} collective-permute-done((f32[8,128]{1,0:T(8,128)S(1)}, f32[8,128]{1,0:T(8,128)S(1)}, u32[]{:S(2)}, u32[]{:S(2)}) %collective-permute-start.1) | collective-permute-done | bytes 4128 | tf_op jit(solution)/shard_map/ppermute | solution.py:34
  16.4 2.1 %shard_map.97 = (bf16[128,1408]{1,0:T(8,128)(2,1)S(1)}, f32[128,1408]{1,0:T(8,128)S(1)}, f32[1,1408]{1,0:T(1,128)S(1)}, bf16[1408,128]{1,0:T(8,128)(2,1)S(1)}) custom-call(s32[1,2]{1,0:T(1,128)S(1)} %copy-done.3, s32[2]{0:T(128)S(1)} %copy-done.4, bf16[2,128,1408]{2,1,0:T(8,128)(2,1)S(1)} %copy-done, f32[1,1408]{1,0:T(1,128)S(1)} %reshape.9.gain_ref, ...), custom_call_target="tpu_custom_call" | custom-call | flops 1000 | bytes 1000 | tf_op jit(solution)/shard_map/pallas_call | solution.py:18
  18.4 1.4 %collective-permute-start.2 = (bf16[1408,128]{1,0:T(8,128)(2,1)S(1)}, bf16[1408,128]{1,0:T(8,128)(2,1)S(1)}, u32[]{:S(2)}, u32[]{:S(2)}) collective-permute-start(bf16[1408,128]{1,0:T(8,128)(2,1)S(1)} %get-tuple-element.60), channel_id=1, source_target_pairs={{0,17},{1,16},{16,1},{17,0},{2,19},{3,18},{18,3},{19,2},{4,21},{5,... | collective-permute-start | bytes 1081352 | tf_op jit(solution)/shard_map/ppermute | solution.py:34
  19.8 0.0 collective-permute-done.5.refs_3_
  19.8 1.1 %collective-permute-done.6.refs_2_ = bf16[704,128]{1,0:T(8,128)(2,1)S(1)} collective-permute-done((bf16[704,128]{1,0:T(8,128)(2,1)S(1)}, bf16[704,128]{1,0:T(8,128)(2,1)S(1)}, u32[]{:S(2)}, u32[]{:S(2)}) %collective-permute-start.6) | collective-permute-done | bytes 180256 | tf_op jit(solution)/shard_map/ppermute | solution.py:374
  21.0 0.0 collective-permute-done.7.refs_1_
  21.0 2.4 %collective-permute-start.10 = (bf16[128,1408]{1,0:T(8,128)(2,1)S(1)}, bf16[128,1408]{1,0:T(8,128)(2,1)S(1)}, u32[]{:S(2)}, u32[]{:S(2)}) collective-permute-start(bf16[128,1408]{1,0:T(8,128)(2,1)S(1)} %get-tuple-element.76.db_ref.refs_0_), channel_id=1, source_target_pairs={{0,6},{2,4},{4,2},{6,0},{8,14},{10,12},{12,10},{14,8},{1,7},{3,5},... | collective-permute-start | bytes 1081352 | tf_op jit(solution)/shard_map/ppermute | solution.py:374
  23.4 0.4 collective-permute-start.9
  23.8 0.6 collective-permute-start.8
  24.5 1.2 %shard_map.98.kept_ref = f32[1408,128]{1,0:T(8,128)S(1)} custom-call(bf16[128,1408]{1,0:T(8,128)(2,1)S(1)} %get-tuple-element.76.db_ref.refs_0_, bf16[2816,1408]{1,0:T(8,128)(2,1)S(1)} %shard_map.94.weight_ref), custom_call_target="tpu_custom_call" | custom-call | flops 1000 | bytes 1000 | tf_op jit(solution)/shard_map/pallas_call | solution.py:18
  25.6 3.0 %collective-permute-done.2.sent_ref = bf16[1408,128]{1,0:T(8,128)(2,1)S(1)} collective-permute-done((bf16[1408,128]{1,0:T(8,128)(2,1)S(1)}, bf16[1408,128]{1,0:T(8,128)(2,1)S(1)}, u32[]{:S(2)}, u32[]{:S(2)}) %collective-permute-start.2) | collective-permute-done | bytes 360480 | tf_op jit(solution)/shard_map/ppermute | solution.py:34
  28.6 1.0 %shard_map.99 = (f32[128,1408]{1,0:T(8,128)S(1)}, f32[8,128]{1,0:T(8,128)S(1)}, f32[8,1408]{1,0:T(8,128)S(1)}) custom-call(s32[1,2]{1,0:T(1,128)S(1)} %copy-done.3, s32[2]{0:T(128)S(1)} %copy-done.4, bf16[2,128,1408]{2,1,0:T(8,128)(2,1)S(1)} %copy-done, f32[1,1408]{1,0:T(1,128)S(1)} %reshape.9.gain_ref, f32[128,1408]{1,0:T(8,128)S(1)} %get-tuple-element.57.keep_ref, ...), custom_call_target="tpu_custom_call" | custom-call | flops 1000 | bytes 1000 | tf_op jit(solution)/shard_map/pallas_call | solution.py:18
  29.6 0.8 collective-permute-start.4
  30.4 1.7 %collective-permute-start.3 = (f32[8,128]{1,0:T(8,128)S(1)}, f32[8,128]{1,0:T(8,128)S(1)}, u32[]{:S(2)}, u32[]{:S(2)}) collective-permute-start(f32[8,128]{1,0:T(8,128)S(1)} %get-tuple-element.65.inner_ref), channel_id=1, source_target_pairs={{0,17},{1,16},{16,1},{17,0},{2,19},{3,18},{18,3},{19,2},{4,21},{5,... | collective-permute-start | bytes 12296 | tf_op jit(solution)/shard_map/ppermute | solution.py:34
  32.2 1.3 %collective-permute-done.3.other_ref = f32[8,128]{1,0:T(8,128)S(1)} collective-permute-done((f32[8,128]{1,0:T(8,128)S(1)}, f32[8,128]{1,0:T(8,128)S(1)}, u32[]{:S(2)}, u32[]{:S(2)}) %collective-permute-start.3) | collective-permute-done | bytes 4128 | tf_op jit(solution)/shard_map/ppermute | solution.py:34
  33.5 0.4 shard_map.100
  33.9 0.0 collective-permute-done.4
  34.0 0.0 collective-permute-done.10.refs_3_
  34.0 6.0 %collective-permute-done.9.refs_2_ = bf16[128,1408]{1,0:T(8,128)(2,1)S(1)} collective-permute-done((bf16[128,1408]{1,0:T(8,128)(2,1)S(1)}, bf16[128,1408]{1,0:T(8,128)(2,1)S(1)}, u32[]{:S(2)}, u32[]{:S(2)}) %collective-permute-start.9) | collective-permute-done | bytes 360480 | tf_op jit(solution)/shard_map/ppermute | solution.py:374
  39.9 0.0 collective-permute-done.8.refs_1_
  39.9 1.0 %collective-permute-start.11 = (bf16[4,704,128]{2,1,0:T(8,128)(2,1)S(1)}, bf16[4,704,128]{2,1,0:T(8,128)(2,1)S(1)}, u32[]{:S(2)}, u32[]{:S(2)}) collective-permute-start(bf16[4,704,128]{2,1,0:T(8,128)(2,1)S(1)} %shard_map.101.own_ref), channel_id=1, source_target_pairs={{0,17},{1,16},{16,1},{17,0},{2,19},{3,18},{18,3},{19,2},{4,21},{5,... | collective-permute-start | bytes 2162696 | tf_op jit(solution)/shard_map/ppermute | solution.py:34
  40.9 2.5 %collective-permute-start.14 = (bf16[128,1408]{1,0:T(8,128)(2,1)S(1)}, bf16[128,1408]{1,0:T(8,128)(2,1)S(1)}, u32[]{:S(2)}, u32[]{:S(2)}) collective-permute-start(bf16[128,1408]{1,0:T(8,128)(2,1)S(1)} %get-tuple-element.88.refs_0_), channel_id=1, source_target_pairs={{0,6},{2,4},{4,2},{6,0},{8,14},{10,12},{12,10},{14,8},{1,7},{3,5},... | collective-permute-start | bytes 1081352 | tf_op jit(solution)/shard_map/ppermute | solution.py:374
  43.5 0.4 collective-permute-start.13
  43.9 0.5 collective-permute-start.12
  44.4 1.6 %collective-permute-start.15 = (f32[8,1408]{1,0:T(8,128)S(1)}, f32[8,1408]{1,0:T(8,128)S(1)}, u32[]{:S(2)}, u32[]{:S(2)}) collective-permute-start(f32[8,1408]{1,0:T(8,128)S(1)} %add.9), channel_id=1, source_target_pairs={{0,4},{2,6},{4,0},{6,2},{8,12},{10,14},{12,8},{14,10},{1,5},{3,7},... | collective-permute-start | bytes 135176 | tf_op jit(solution)/shard_map/ppermute | solution.py:374
  46.0 12.3 %collective-permute-done.11.other_ref = bf16[4,704,128]{2,1,0:T(8,128)(2,1)S(1)} collective-permute-done((bf16[4,704,128]{2,1,0:T(8,128)(2,1)S(1)}, bf16[4,704,128]{2,1,0:T(8,128)(2,1)S(1)}, u32[]{:S(2)}, u32[]{:S(2)}) %collective-permute-start.11) | collective-permute-done | bytes 720928 | tf_op jit(solution)/shard_map/ppermute | solution.py:34
  58.3 0.4 shard_map.102.left_ref
  58.7 1.4 %shard_map.103 = (f32[352,1408]{1,0:T(8,128)S(1)}, f32[352,1408]{1,0:T(8,128)S(1)}) custom-call(bf16[704,1024]{1,0:T(8,128)(2,1)S(1)} %shard_map.102.left_ref, bf16[128,1408]{1,0:T(8,128)(2,1)S(1)} %get-tuple-element.76.db_ref.refs_0_, bf16[128,1408]{1,0:T(8,128)(2,1)S(1)} %collective-permute-done.8.refs_1_, ...), custom_call_target="tpu_custom_call" | custom-call | flops 1000 | bytes 1000 | tf_op jit(solution)/shard_map/pallas_call | solution.py:18
  60.1 1.3 %collective-permute-done.15 = f32[8,1408]{1,0:T(8,128)S(1)} collective-permute-done((f32[8,1408]{1,0:T(8,128)S(1)}, f32[8,1408]{1,0:T(8,128)S(1)}, u32[]{:S(2)}, u32[]{:S(2)}) %collective-permute-start.15) | collective-permute-done | bytes 45088 | tf_op jit(solution)/shard_map/ppermute | solution.py:374
  61.4 0.0 collective-permute-done.14.refs_3_
  61.4 0.0 collective-permute-done.13.refs_2_
  61.4 0.0 collective-permute-done.12.refs_1_
  61.4 0.8 shard_map.105
  62.2 0.1 collective-permute-start.16
  62.3 0.8 shard_map.104
  63.1 0.6 collective-permute-start.17
  63.7 1.3 %collective-permute-done.16.other_ref = f32[352,768]{1,0:T(8,128)S(1)} collective-permute-done((f32[352,768]{1,0:T(8,128)S(1)}, f32[352,768]{1,0:T(8,128)S(1)}, u32[]{:S(2)}, u32[]{:S(2)}) %collective-permute-start.16) | collective-permute-done | bytes 1081376 | tf_op jit(solution)/shard_map/ppermute | solution.py:30
  65.0 0.1 shard_map.106
  65.1 0.2 collective-permute-start.19
  65.3 2.6 %collective-permute-start.22 = (bf16[176,768]{1,0:T(8,128)(2,1)S(1)}, bf16[176,768]{1,0:T(8,128)(2,1)S(1)}, u32[]{:S(2)}, u32[]{:S(2)}) collective-permute-start(bf16[176,768]{1,0:T(8,128)(2,1)S(1)} %get-tuple-element.97), channel_id=1, source_target_pairs={{0,8},{2,10},{4,12},{6,14},{8,0},{10,2},{12,4},{14,6},{1,9},{3,11}... | collective-permute-start | bytes 811016 | tf_op jit(solution)/shard_map/ppermute | solution.py:374
  67.9 0.0 collective-permute-done.17.other_ref
  67.9 0.1 shard_map.107
  68.1 1.0 %collective-permute-start.18 = (bf16[176,640]{1,0:T(8,128)(2,1)S(1)}, bf16[176,640]{1,0:T(8,128)(2,1)S(1)}, u32[]{:S(2)}, u32[]{:S(2)}) collective-permute-start(bf16[176,640]{1,0:T(8,128)(2,1)S(1)} %get-tuple-element.100), channel_id=1, source_target_pairs={{0,8},{2,10},{4,12},{6,14},{8,0},{10,2},{12,4},{14,6},{1,9},{3,11}... | collective-permute-start | bytes 675848 | tf_op jit(solution)/shard_map/ppermute | solution.py:374
  69.1 0.6 collective-permute-start.20
  69.7 3.4 %collective-permute-done.20 = f32[8,1408]{1,0:T(8,128)S(1)} collective-permute-done((f32[8,1408]{1,0:T(8,128)S(1)}, f32[8,1408]{1,0:T(8,128)S(1)}, u32[]{:S(2)}, u32[]{:S(2)}) %collective-permute-start.20) | collective-permute-done | bytes 45088 | tf_op jit(solution)/shard_map/ppermute | solution.py:374
  73.1 2.0 %collective-permute-start.21 = (f32[8,1408]{1,0:T(8,128)S(1)}, f32[8,1408]{1,0:T(8,128)S(1)}, u32[]{:S(2)}, u32[]{:S(2)}) collective-permute-start(f32[8,1408]{1,0:T(8,128)S(1)} %add.11.refs_0_), channel_id=1, source_target_pairs={{0,8},{2,10},{4,12},{6,14},{8,0},{10,2},{12,4},{14,6},{1,9},{3,11}... | collective-permute-start | bytes 135176 | tf_op jit(solution)/shard_map/ppermute | solution.py:374
  75.2 0.0 collective-permute-done.19.other_ref
  75.2 1.7 %shard_map.108 = f32[2,128,1408]{2,1,0:T(8,128)} custom-call(s32[1,2]{1,0:T(1,128)S(1)} %copy-done.3, f32[128,1408]{1,0:T(8,128)S(1)} %get-tuple-element.102.total_ref, f32[128,1408]{1,0:T(8,128)S(1)} %collective-permute-done.19.other_ref), custom_call_target="tpu_custom_call" | custom-call | flops 1000 | bytes 1000 | tf_op jit(solution)/shard_map/pallas_call | solution.py:18
  76.9 15.0 %collective-permute-done.18.refs_5_ = bf16[176,640]{1,0:T(8,128)(2,1)S(1)} collective-permute-done((bf16[176,640]{1,0:T(8,128)(2,1)S(1)}, bf16[176,640]{1,0:T(8,128)(2,1)S(1)}, u32[]{:S(2)}, u32[]{:S(2)}) %collective-permute-start.18) | collective-permute-done | bytes 225312 | tf_op jit(solution)/shard_map/ppermute | solution.py:374
  91.9 0.5 collective-permute-done.21.refs_1_
  92.4 0.0 collective-permute-done.22.refs_3_
  92.4 1.0 %shard_map.109 = (f32[176,1408]{1,0:T(8,128)}, f32[1408]{0:T(1024)}) custom-call(f32[8,1408]{1,0:T(8,128)S(1)} %add.11.refs_0_, f32[8,1408]{1,0:T(8,128)S(1)} %collective-permute-done.21.refs_1_, f32[176,768]{1,0:T(8,128)S(1)} %get-tuple-element.106.refs_2_, bf16[176,768]{1,0:T(8,128)(2,1)S(1)} %collective-permute-done.22.refs_3_, ...), custom_call_target="tpu_custom_call" | custom-call | flops 1000 | bytes 1000 | tf_op jit(solution)/shard_map/pallas_call | solution.py:18
  (14 shorter events, 0.1 us)
Async XLA Ops:
  0.6 3.6 %copy-start.3 = (s32[1,2]{1,0:T(1,128)S(1)}, s32[1,2]{1,0:T(1,128)}, u32[]{:S(2)}) copy-start(s32[1,2]{1,0:T(1,128)} %order_ref.9) | copy-start | bytes 28
  0.6 3.6 %copy-start.2 = (bf16[2,128,1408]{2,1,0:T(8,128)(2,1)S(1)}, bf16[2,128,1408]{2,1,0:T(8,128)(2,1)}, u32[]{:S(2)}) copy-start(bf16[2,128,1408]{2,1,0:T(8,128)(2,1)} %inj_ref.1) | copy-start | bytes 2162692
  0.7 3.9 %copy-start.1 = (bf16[1,2,128,2816]{3,2,1,0:T(8,128)(2,1)S(1)}, bf16[1,2,128,2816]{3,2,1,0:T(8,128)(2,1)}, u32[]{:S(2)}) copy-start(bf16[1,2,128,2816]{3,2,1,0:T(8,128)(2,1)} %param.7) | copy-start | bytes 4325380
  4.6 7.8 %copy-start.5 = (f32[1408]{0:T(1024)S(1)}, f32[1408]{0:T(1024)}, u32[]{:S(2)}) copy-start(f32[1408]{0:T(1024)} %param.10) | copy-start | bytes 16900
  4.6 7.8 %copy-start = (bf16[2,128,1408]{2,1,0:T(8,128)(2,1)S(1)}, bf16[2,128,1408]{2,1,0:T(8,128)(2,1)}, u32[]{:S(2)}) copy-start(bf16[2,128,1408]{2,1,0:T(8,128)(2,1)} %cot_ref.5) | copy-start | bytes 2162692
  7.6 8.8 %copy-start.4 = (s32[2]{0:T(128)S(1)}, s32[2]{0:T(128)}, u32[]{:S(2)}) copy-start(s32[2]{0:T(128)} %exits_ref.3) | copy-start | bytes 28
  7.6 4.8 %collective-permute-start = (f32[128,1408]{1,0:T(8,128)S(1)}, f32[128,1408]{1,0:T(8,128)S(1)}, u32[]{:S(2)}, u32[]{:S(2)}) collective-permute-start(f32[128,1408]{1,0:T(8,128)S(1)} %get-tuple-element.58), channel_id=1, source_target_pairs={{0,16},{16,0},{1,17},{17,1},{2,18},{18,2},{3,19},{19,3},{4,20},{20... | collective-permute-start | bytes 2162696 | tf_op jit(solution)/shard_map/ppermute | solution.py:30
  8.1 11.7 %collective-permute-start.5 = (bf16[704,128]{1,0:T(8,128)(2,1)S(1)}, bf16[704,128]{1,0:T(8,128)(2,1)S(1)}, u32[]{:S(2)}, u32[]{:S(2)}) collective-permute-start(bf16[704,128]{1,0:T(8,128)(2,1)S(1)} %get-tuple-element.70), channel_id=1, source_target_pairs={{0,6},{2,4},{4,2},{6,0},{8,14},{10,12},{12,10},{14,8},{1,7},{3,5},... | collective-permute-start | bytes 540680 | tf_op jit(solution)/shard_map/ppermute | solution.py:374
  11.7 9.2 %collective-permute-start.6 = (bf16[704,128]{1,0:T(8,128)(2,1)S(1)}, bf16[704,128]{1,0:T(8,128)(2,1)S(1)}, u32[]{:S(2)}, u32[]{:S(2)}) collective-permute-start(bf16[704,128]{1,0:T(8,128)(2,1)S(1)} %get-tuple-element.71), channel_id=1, source_target_pairs={{0,4},{2,6},{4,0},{6,2},{8,12},{10,14},{12,8},{14,10},{1,5},{3,7},... | collective-permute-start | bytes 540680 | tf_op jit(solution)/shard_map/ppermute | solution.py:374
  12.2 8.8 %collective-permute-start.7 = (bf16[704,128]{1,0:T(8,128)(2,1)S(1)}, bf16[704,128]{1,0:T(8,128)(2,1)S(1)}, u32[]{:S(2)}, u32[]{:S(2)}) collective-permute-start(bf16[704,128]{1,0:T(8,128)(2,1)S(1)} %get-tuple-element.72), channel_id=1, source_target_pairs={{0,2},{2,0},{4,6},{6,4},{8,10},{10,8},{12,14},{14,12},{1,3},{3,1},... | collective-permute-start | bytes 540680 | tf_op jit(solution)/shard_map/ppermute | solution.py:374
  13.3 3.1 %collective-permute-start.1 = (f32[8,128]{1,0:T(8,128)S(1)}, f32[8,128]{1,0:T(8,128)S(1)}, u32[]{:S(2)}, u32[]{:S(2)}) collective-permute-start(f32[8,128]{1,0:T(8,128)S(1)} %shard_map.96.sums_ref), channel_id=1, source_target_pairs={{0,17},{1,16},{16,1},{17,0},{2,19},{3,18},{18,3},{19,2},{4,21},{5,... | collective-permute-start | bytes 12296 | tf_op jit(solution)/shard_map/ppermute | solution.py:34
  18.4 10.2 %collective-permute-start.2 = (bf16[1408,128]{1,0:T(8,128)(2,1)S(1)}, bf16[1408,128]{1,0:T(8,128)(2,1)S(1)}, u32[]{:S(2)}, u32[]{:S(2)}) collective-permute-start(bf16[1408,128]{1,0:T(8,128)(2,1)S(1)} %get-tuple-element.60), channel_id=1, source_target_pairs={{0,17},{1,16},{16,1},{17,0},{2,19},{3,18},{18,3},{19,2},{4,21},{5,... | collective-permute-start | bytes 1081352 | tf_op jit(solution)/shard_map/ppermute | solution.py:34
  21.0 13.0 %collective-permute-start.10 = (bf16[128,1408]{1,0:T(8,128)(2,1)S(1)}, bf16[128,1408]{1,0:T(8,128)(2,1)S(1)}, u32[]{:S(2)}, u32[]{:S(2)}) collective-permute-start(bf16[128,1408]{1,0:T(8,128)(2,1)S(1)} %get-tuple-element.76.db_ref.refs_0_), channel_id=1, source_target_pairs={{0,6},{2,4},{4,2},{6,0},{8,14},{10,12},{12,10},{14,8},{1,7},{3,5},... | collective-permute-start | bytes 1081352 | tf_op jit(solution)/shard_map/ppermute | solution.py:374
  23.4 16.5 %collective-permute-start.9 = (bf16[128,1408]{1,0:T(8,128)(2,1)S(1)}, bf16[128,1408]{1,0:T(8,128)(2,1)S(1)}, u32[]{:S(2)}, u32[]{:S(2)}) collective-permute-start(bf16[128,1408]{1,0:T(8,128)(2,1)S(1)} %get-tuple-element.76.db_ref.refs_0_), channel_id=1, source_target_pairs={{0,4},{2,6},{4,0},{6,2},{8,12},{10,14},{12,8},{14,10},{1,5},{3,7},... | collective-permute-start | bytes 1081352 | tf_op jit(solution)/shard_map/ppermute | solution.py:374
  23.8 16.1 %collective-permute-start.8 = (bf16[128,1408]{1,0:T(8,128)(2,1)S(1)}, bf16[128,1408]{1,0:T(8,128)(2,1)S(1)}, u32[]{:S(2)}, u32[]{:S(2)}) collective-permute-start(bf16[128,1408]{1,0:T(8,128)(2,1)S(1)} %get-tuple-element.76.db_ref.refs_0_), channel_id=1, source_target_pairs={{0,2},{2,0},{4,6},{6,4},{8,10},{10,8},{12,14},{14,12},{1,3},{3,1},... | collective-permute-start | bytes 1081352 | tf_op jit(solution)/shard_map/ppermute | solution.py:374
  29.6 4.3 %collective-permute-start.4 = (f32[8,1408]{1,0:T(8,128)S(1)}, f32[8,1408]{1,0:T(8,128)S(1)}, u32[]{:S(2)}, u32[]{:S(2)}) collective-permute-start(f32[8,1408]{1,0:T(8,128)S(1)} %get-tuple-element.68), channel_id=1, source_target_pairs={{0,16},{16,0},{1,17},{17,1},{2,18},{18,2},{3,19},{19,3},{4,20},{20... | collective-permute-start | bytes 135176 | tf_op jit(solution)/shard_map/ppermute | solution.py:30
  30.4 3.0 %collective-permute-start.3 = (f32[8,128]{1,0:T(8,128)S(1)}, f32[8,128]{1,0:T(8,128)S(1)}, u32[]{:S(2)}, u32[]{:S(2)}) collective-permute-start(f32[8,128]{1,0:T(8,128)S(1)} %get-tuple-element.65.inner_ref), channel_id=1, source_target_pairs={{0,17},{1,16},{16,1},{17,0},{2,19},{3,18},{18,3},{19,2},{4,21},{5,... | collective-permute-start | bytes 12296 | tf_op jit(solution)/shard_map/ppermute | solution.py:34
  39.9 18.4 %collective-permute-start.11 = (bf16[4,704,128]{2,1,0:T(8,128)(2,1)S(1)}, bf16[4,704,128]{2,1,0:T(8,128)(2,1)S(1)}, u32[]{:S(2)}, u32[]{:S(2)}) collective-permute-start(bf16[4,704,128]{2,1,0:T(8,128)(2,1)S(1)} %shard_map.101.own_ref), channel_id=1, source_target_pairs={{0,17},{1,16},{16,1},{17,0},{2,19},{3,18},{18,3},{19,2},{4,21},{5,... | collective-permute-start | bytes 2162696 | tf_op jit(solution)/shard_map/ppermute | solution.py:34
  40.9 20.5 %collective-permute-start.14 = (bf16[128,1408]{1,0:T(8,128)(2,1)S(1)}, bf16[128,1408]{1,0:T(8,128)(2,1)S(1)}, u32[]{:S(2)}, u32[]{:S(2)}) collective-permute-start(bf16[128,1408]{1,0:T(8,128)(2,1)S(1)} %get-tuple-element.88.refs_0_), channel_id=1, source_target_pairs={{0,6},{2,4},{4,2},{6,0},{8,14},{10,12},{12,10},{14,8},{1,7},{3,5},... | collective-permute-start | bytes 1081352 | tf_op jit(solution)/shard_map/ppermute | solution.py:374
  43.5 18.0 %collective-permute-start.13 = (bf16[128,1408]{1,0:T(8,128)(2,1)S(1)}, bf16[128,1408]{1,0:T(8,128)(2,1)S(1)}, u32[]{:S(2)}, u32[]{:S(2)}) collective-permute-start(bf16[128,1408]{1,0:T(8,128)(2,1)S(1)} %get-tuple-element.88.refs_0_), channel_id=1, source_target_pairs={{0,4},{2,6},{4,0},{6,2},{8,12},{10,14},{12,8},{14,10},{1,5},{3,7},... | collective-permute-start | bytes 1081352 | tf_op jit(solution)/shard_map/ppermute | solution.py:374
  43.9 17.5 %collective-permute-start.12 = (bf16[128,1408]{1,0:T(8,128)(2,1)S(1)}, bf16[128,1408]{1,0:T(8,128)(2,1)S(1)}, u32[]{:S(2)}, u32[]{:S(2)}) collective-permute-start(bf16[128,1408]{1,0:T(8,128)(2,1)S(1)} %get-tuple-element.88.refs_0_), channel_id=1, source_target_pairs={{0,2},{2,0},{4,6},{6,4},{8,10},{10,8},{12,14},{14,12},{1,3},{3,1},... | collective-permute-start | bytes 1081352 | tf_op jit(solution)/shard_map/ppermute | solution.py:374
  44.4 17.0 %collective-permute-start.15 = (f32[8,1408]{1,0:T(8,128)S(1)}, f32[8,1408]{1,0:T(8,128)S(1)}, u32[]{:S(2)}, u32[]{:S(2)}) collective-permute-start(f32[8,1408]{1,0:T(8,128)S(1)} %add.9), channel_id=1, source_target_pairs={{0,4},{2,6},{4,0},{6,2},{8,12},{10,14},{12,8},{14,10},{1,5},{3,7},... | collective-permute-start | bytes 135176 | tf_op jit(solution)/shard_map/ppermute | solution.py:374
  62.2 2.8 %collective-permute-start.16 = (f32[352,768]{1,0:T(8,128)S(1)}, f32[352,768]{1,0:T(8,128)S(1)}, u32[]{:S(2)}, u32[]{:S(2)}) collective-permute-start(f32[352,768]{1,0:T(8,128)S(1)} %get-tuple-element.96), channel_id=1, source_target_pairs={{0,16},{16,0},{1,17},{17,1},{2,18},{18,2},{3,19},{19,3},{4,20},{20... | collective-permute-start | bytes 3244040 | tf_op jit(solution)/shard_map/ppermute | solution.py:30
  63.1 4.8 %collective-permute-start.17 = (f32[352,640]{1,0:T(8,128)S(1)}, f32[352,640]{1,0:T(8,128)S(1)}, u32[]{:S(2)}, u32[]{:S(2)}) collective-permute-start(f32[352,640]{1,0:T(8,128)S(1)} %get-tuple-element.99), channel_id=1, source_target_pairs={{0,16},{16,0},{1,17},{17,1},{2,18},{18,2},{3,19},{19,3},{4,20},{20... | collective-permute-start | bytes 2703368 | tf_op jit(solution)/shard_map/ppermute | solution.py:30
  65.1 10.1 %collective-permute-start.19 = (f32[128,1408]{1,0:T(8,128)S(1)}, f32[128,1408]{1,0:T(8,128)S(1)}, u32[]{:S(2)}, u32[]{:S(2)}) collective-permute-start(f32[128,1408]{1,0:T(8,128)S(1)} %get-tuple-element.102.total_ref), channel_id=1, source_target_pairs={{0,16},{16,0},{1,17},{17,1},{2,18},{18,2},{3,19},{19,3},{4,20},{20... | collective-permute-start | bytes 2162696 | tf_op jit(solution)/shard_map/ppermute | solution.py:30
  65.3 27.0 %collective-permute-start.22 = (bf16[176,768]{1,0:T(8,128)(2,1)S(1)}, bf16[176,768]{1,0:T(8,128)(2,1)S(1)}, u32[]{:S(2)}, u32[]{:S(2)}) collective-permute-start(bf16[176,768]{1,0:T(8,128)(2,1)S(1)} %get-tuple-element.97), channel_id=1, source_target_pairs={{0,8},{2,10},{4,12},{6,14},{8,0},{10,2},{12,4},{14,6},{1,9},{3,11}... | collective-permute-start | bytes 811016 | tf_op jit(solution)/shard_map/ppermute | solution.py:374
  68.1 23.8 %collective-permute-start.18 = (bf16[176,640]{1,0:T(8,128)(2,1)S(1)}, bf16[176,640]{1,0:T(8,128)(2,1)S(1)}, u32[]{:S(2)}, u32[]{:S(2)}) collective-permute-start(bf16[176,640]{1,0:T(8,128)(2,1)S(1)} %get-tuple-element.100), channel_id=1, source_target_pairs={{0,8},{2,10},{4,12},{6,14},{8,0},{10,2},{12,4},{14,6},{1,9},{3,11}... | collective-permute-start | bytes 675848 | tf_op jit(solution)/shard_map/ppermute | solution.py:374
  69.1 4.0 %collective-permute-start.20 = (f32[8,1408]{1,0:T(8,128)S(1)}, f32[8,1408]{1,0:T(8,128)S(1)}, u32[]{:S(2)}, u32[]{:S(2)}) collective-permute-start(f32[8,1408]{1,0:T(8,128)S(1)} %add.10), channel_id=1, source_target_pairs={{0,2},{2,0},{4,6},{6,4},{8,10},{10,8},{12,14},{14,12},{1,3},{3,1},... | collective-permute-start | bytes 135176 | tf_op jit(solution)/shard_map/ppermute | solution.py:374
  73.1 19.2 %collective-permute-start.21 = (f32[8,1408]{1,0:T(8,128)S(1)}, f32[8,1408]{1,0:T(8,128)S(1)}, u32[]{:S(2)}, u32[]{:S(2)}) collective-permute-start(f32[8,1408]{1,0:T(8,128)S(1)} %add.11.refs_0_), channel_id=1, source_target_pairs={{0,8},{2,10},{4,12},{6,14},{8,0},{10,2},{12,4},{14,6},{1,9},{3,11}... | collective-permute-start | bytes 135176 | tf_op jit(solution)/shard_map/ppermute | solution.py:374
